TPU v7x, 32 devices: a whole 2x2x4 slice. The times are simulated.
32 devices in a mesh: pop: 8 (over z, y), col: 4 (over x, core).
Axes of the slice: x: 2, y: 2, z: 4, core: 2. Of those that a mesh axis runs over, the one named last changes fastest.
Arguments:
- weight: float32 [2304, 16384], P('pop', 'col'), may hold values from -3 to 3
- row_factors: bfloat16 [2304, 768], P(None, 'pop'), may hold values from -6 to 6
- col_factors: bfloat16 [768, 16384], P('pop', 'col'), may hold values from -6 to 6
- fitness_ranks: int32 [768], P('pop'), may hold values from 0 to 767, each once
Outputs:
- new_weight: float32 [2304, 16384], P('pop', 'col')
Inputs may be any that keep to these rules, and one draw needn't show every extreme that they name: fitness_ranks holds each of 0 to 767 exactly once.
All inputs are finite; a program needn't handle non-finite values.
Results may differ from a plain program's by a relative error of at most 0.0026.
Values may be sent and summed in bfloat16 or wider, within the bound.
A program may use at most 64 MiB of HBM per device.

v0:
```python
import functools
import math

import jax
import jax.numpy as jnp
from jax import lax
from jax.experimental import pallas as pl
from jax.experimental.pallas import tpu as pltpu
from jax.sharding import PartitionSpec as P

MESH = pl.DeviceIdType.MESH
WIDTH = 256
LAG = 2


def kernel(zc, members, share, ranks_ref, rft_ref, col_ref, w_ref, own,
           shaped, rf_ref, colv, g, rfl, ysend, yrecv, wv, sem_in, left_send, left_recv, right_send, right_recv,
           rf_send, rf_recv, x_send, x_recv, fwd_send, fwd_recv, y_send, y_recv):
    mb, cols = colv.shape
    kb = rf_ref.shape[1]
    rows = own.shape[0]
    nch = cols // WIDTH
    scale = 3.0 / math.sqrt(members)
    me = lax.axis_index("pop")
    c = lax.axis_index("col")
    z, y = me // 2, me % 2
    part = c % share
    piece_rows = 2 * rows // share
    core = c % 2
    mate = c + 1 - 2 * core
    x_mate = c + 2 - 4 * (part // 2)
    partner = me + 1 - 2 * y

    col_in = pltpu.make_async_copy(col_ref, colv, sem_in.at[0])
    w_in = pltpu.make_async_copy(w_ref, wv, sem_in.at[1])
    col_in.start()

    barrier = pltpu.get_barrier_semaphore()
    for dz in range(1, zc):
        other = lax.rem(z + dz, zc) * 2 + y
        pl.semaphore_signal(barrier, inc=1, device_id=(other, c), device_id_type=MESH)
    pl.semaphore_signal(barrier, inc=1, device_id=(partner, c), device_id_type=MESH)
    pl.semaphore_signal(barrier, inc=1, device_id=(me, mate), device_id_type=MESH)
    if share == 4:
        pl.semaphore_signal(barrier, inc=1, device_id=(me, x_mate), device_id_type=MESH)

    flat = jnp.broadcast_to(ranks_ref[...].astype(jnp.float32), (mb, mb))
    eye = lax.broadcasted_iota(jnp.int32, (mb, mb), 0) == lax.broadcasted_iota(jnp.int32, (mb, mb), 1)
    rank = jnp.sum(jnp.where(eye, flat, 0.0), axis=1, keepdims=True)
    shaped[...] = jnp.broadcast_to(rank / (members - 1) - 0.5, shaped.shape)
    for at in range(0, rf_ref.shape[0], 128):
        tile = rft_ref[:, at:at + 128].astype(jnp.float32)
        if kb > mb:
            tile = jnp.concatenate([tile, jnp.zeros((kb - mb, 128), jnp.float32)], axis=0)
        rf_ref[at:at + 128, :] = tile.T.astype(jnp.bfloat16)
    col_in.wait()
    pl.semaphore_wait(barrier, zc + 1 + (share == 4))

    def chunk(j):
        return pl.ds(pl.multiple_of(j * WIDTH, WIDTH), WIDTH)

    def block_copy(b, j, send, recv, target):
        piece = g.at[j, b, pl.ds(0, mb), :]
        return pltpu.make_async_remote_copy(
            src_ref=piece, dst_ref=piece, send_sem=send, recv_sem=recv,
            device_id=(target * 2 + y, c), device_id_type=MESH)

    def left_copy(d, j):
        return block_copy(z + d, j, left_send.at[d, j], left_recv.at[d + 1, j], z - 1)

    def right_copy(d, j):
        return block_copy(z - d, j, right_send.at[d, j], right_recv.at[d + 1, j], z + 1)

    def arrival(b, j, recv):
        piece = g.at[j, b, pl.ds(0, mb), :]
        return pltpu.make_async_copy(piece, piece, recv)

    def rf_rows(index):
        return pl.ds(pl.multiple_of(index * piece_rows, 16), piece_rows)

    def rf_copy(dz):
        to = lax.rem(z + dz, zc)
        return pltpu.make_async_remote_copy(
            src_ref=rf_ref.at[rf_rows(to * share + part)], dst_ref=rfl.at[z, rf_rows(part)],
            send_sem=rf_send.at[dz], recv_sem=rf_recv.at[dz],
            device_id=(to * 2 + y, c), device_id_type=MESH)

    def pass_on(dz, index, send, recv, target):
        piece = rfl.at[lax.rem(z + zc - dz, zc), rf_rows(index)]
        return pltpu.make_async_remote_copy(
            src_ref=piece, dst_ref=piece, send_sem=send, recv_sem=recv,
            device_id=(me, target), device_id_type=MESH)

    def x_copy(dz):
        return pass_on(dz, part, x_send.at[dz], x_recv.at[dz], x_mate)

    def fwd_copy(dz, k):
        index = part if k == 0 else lax.rem(part + 2, share)
        return pass_on(dz, index, fwd_send.at[dz, k], fwd_recv.at[dz, k], mate)

    def landed(dz, index, recv):
        piece = rfl.at[lax.rem(z + zc - dz, zc), rf_rows(index)]
        return pltpu.make_async_copy(piece, piece, recv)

    def y_copy(j):
        return pltpu.make_async_remote_copy(
            src_ref=ysend.at[j], dst_ref=yrecv.at[j],
            send_sem=y_send.at[j], recv_sem=y_recv.at[j],
            device_id=(partner, c), device_id_type=MESH)

    for dz in range(1, zc):
        rf_copy(dz).start()
    w_in.start()

    def lhs(which):
        at = pl.ds(pl.multiple_of(which * rows, 16), rows)
        return jnp.concatenate([rfl[o, at, :] for o in range(zc)], axis=1)

    def tick(t, carry):
        @pl.when(t < nch)
        def _():
            own_part = shaped[:, 0:1] * colv[:, chunk(t)].astype(jnp.float32)
            g[t, z, pl.ds(0, mb), :] = own_part.astype(jnp.bfloat16)

            @pl.when(z > 0)
            def _():
                left_copy(0, t).start()

            @pl.when(z < zc - 1)
            def _():
                right_copy(0, t).start()

        @pl.when(t == 0)
        def _():
            if kb > mb:
                g[:, :, pl.ds(mb, kb - mb), :] = jnp.zeros((nch, zc, kb - mb, WIDTH), jnp.bfloat16)
            rfl[z] = rf_ref[pl.ds(pl.multiple_of(z * 2 * rows, 16), 2 * rows), :]

        for d in range(1, zc):
            j = t - d

            @pl.when((j >= 0) & (j < nch))
            def _():
                @pl.when(z + d < zc)
                def _():
                    arrival(z + d, j, left_recv.at[d, j]).wait()
                    if d < zc - 1:
                        @pl.when(z > 0)
                        def _():
                            left_copy(d, j).start()

                @pl.when(z - d >= 0)
                def _():
                    arrival(z - d, j, right_recv.at[d, j]).wait()
                    if d < zc - 1:
                        @pl.when(z < zc - 1)
                        def _():
                            right_copy(d, j).start()

        @pl.when(t == 1)
        def _():
            for dz in range(1, zc):
                rf_copy(dz).wait_recv()
                if share == 4:
                    x_copy(dz).start()
                fwd_copy(dz, 0).start()

        jc = t - (zc - 1)

        @pl.when(jc == 0)
        def _():
            mate_part = part + 1 - 2 * core
            if share == 4:
                for dz in range(1, zc):
                    landed(dz, lax.rem(part + 2, share), x_recv.at[dz]).wait()
                    fwd_copy(dz, 1).start()
            for dz in range(1, zc):
                landed(dz, mate_part, fwd_recv.at[dz, 0]).wait()
            if share == 4:
                for dz in range(1, zc):
                    landed(dz, lax.rem(mate_part + 2, share), fwd_recv.at[dz, 1]).wait()

        @pl.when((jc >= 0) & (jc < nch))
        def _():
            at = chunk(jc)
            rhs = g[jc].reshape(zc * kb, WIDTH)
            ysend[jc] = jnp.dot(lhs(1 - y), rhs, preferred_element_type=jnp.float32).astype(jnp.bfloat16)
            y_copy(jc).start()
            own[:, at] = jnp.dot(lhs(y), rhs, preferred_element_type=jnp.float32)

        jf = jc - LAG

        @pl.when(jf == 0)
        def _():
            w_in.wait()

        @pl.when(jf >= 0)
        def _():
            at = chunk(jf)
            y_copy(jf).wait_recv()
            own[:, at] = wv[:, at] + scale * (own[:, at] + yrecv[jf].astype(jnp.float32))

        return carry

    lax.fori_loop(0, nch + zc - 1 + LAG, tick, 0)

    def drain(j, carry):
        for d in range(zc - 1):
            @pl.when((z + d < zc) & (z > 0))
            def _():
                left_copy(d, j).wait_send()

            @pl.when((z - d >= 0) & (z < zc - 1))
            def _():
                right_copy(d, j).wait_send()
        y_copy(j).wait_send()
        return carry

    lax.fori_loop(0, nch, drain, 0)
    for dz in range(1, zc):
        rf_copy(dz).wait_send()
        fwd_copy(dz, 0).wait_send()
        if share == 4:
            x_copy(dz).wait_send()
            fwd_copy(dz, 1).wait_send()


def body(weight, row_factors, col_factors, fitness_ranks):
    pop = lax.axis_size("pop")
    mb = fitness_ranks.shape[0]
    members = mb * pop
    zc = pop // 2
    rows, cols = weight.shape
    kb = -(-mb // 128) * 128
    nch = cols // WIDTH
    share = 4 if rows % 32 == 0 and lax.axis_size("col") % 4 == 0 else 2
    anywhere = pl.BlockSpec(memory_space=pl.ANY)
    vmem = pl.BlockSpec(memory_space=pltpu.VMEM)
    dma = pltpu.SemaphoreType.DMA
    return pl.pallas_call(
        functools.partial(kernel, zc, members, share),
        out_shape=pltpu.VMEM((rows, cols), jnp.float32),
        in_specs=[vmem, vmem, anywhere, anywhere],
        out_specs=vmem,
        scratch_shapes=[
            pltpu.VMEM((mb, 128), jnp.float32),
            pltpu.VMEM((row_factors.shape[0], kb), jnp.bfloat16),
            pltpu.VMEM((mb, cols), jnp.bfloat16),
            pltpu.VMEM((nch, zc, kb, WIDTH), jnp.bfloat16),
            pltpu.VMEM((zc, 2 * rows, kb), jnp.bfloat16),
            pltpu.VMEM((nch, rows, WIDTH), jnp.bfloat16),
            pltpu.VMEM((nch, rows, WIDTH), jnp.bfloat16),
            pltpu.VMEM((rows, cols), jnp.float32),
            dma((2,)),
            dma((zc, nch)), dma((zc, nch)), dma((zc, nch)), dma((zc, nch)),
            dma((zc,)), dma((zc,)), dma((zc,)), dma((zc,)), dma((zc, 2)), dma((zc, 2)),
            dma((nch,)), dma((nch,)),
        ],
        compiler_params=pltpu.CompilerParams(
            collective_id=0, has_side_effects=True, vmem_limit_bytes=56 * 1024 * 1024),
        cost_estimate=pl.CostEstimate(
            flops=2 * rows * cols * members, bytes_accessed=8 * rows * cols, transcendentals=0),
    )(fitness_ranks.reshape(1, mb), row_factors.T, col_factors, weight)


def solution(mesh):
    in_specs = (P("pop", "col"), P(None, "pop"), P("pop", "col"), P("pop"))
    out_specs = P("pop", "col")
    return jax.shard_map(body, mesh=mesh, in_specs=in_specs, out_specs=out_specs, check_vma=False)
```

profile of v0, /device:TPU:0, one launch (start us, length us, event | category | flops | bytes accessed | tf_op | source)
XLA Modules:
  0.0 76.5 jit_solution(9269616138581171418)
XLA Ops:
  0.0 74.3 %shard_map.46 = f32[288,4096]{1,0:T(8,128)S(1)} custom-call(s32[1,96]{1,0:T(1,128)} %bitcast.3, bf16[96,2304]{1,0:T(8,128)(2,1)} %bitcast.2, bf16[96,4096]{1,0:T(8,128)(2,1)} %col_ref.1, f32[288,4096]{1,0:T(8,128)} %w_ref.1), custom_call_target="tpu_custom_call" | custom-call | flops 1811939328 | bytes 9437184 | tf_op jit(solution)/shard_map/pallas_call | solution.py:240
  74.3 2.2 %copy.6 = f32[288,4096]{1,0:T(8,128)} copy(f32[288,4096]{1,0:T(8,128)S(1)} %shard_map.46) | data formatting | bytes 9437184
where the time goes:
time: 76.7 us; the launch traced here: 76.5 us
  Pallas kernels  74.3 us (97%)
  local copies, waits for them, and re-layouts  2.19 us (3%)
    pallas_call x1, Pallas kernels, body(): pl.pallas_call(functools.partial(kernel, zc, members, share), out_shape=p...  74.3 us
    unnamed x1, local copies, waits for them, and re-layouts  2.19 us

commit v1 on v0

--- a/solution.py
+++ b/solution.py
@@ -19,7 +19,7 @@
     mb, cols = colv.shape
     kb = rf_ref.shape[1]
     rows = own.shape[0]
-    nch = cols // WIDTH
+    nch = cols // WIDTH + 1
     scale = 3.0 / math.sqrt(members)
     me = lax.axis_index("pop")
     c = lax.axis_index("col")
@@ -56,23 +56,35 @@
     col_in.wait()
     pl.semaphore_wait(barrier, zc + 1 + (share == 4))
 
-    def chunk(j):
-        return pl.ds(pl.multiple_of(j * WIDTH, WIDTH), WIDTH)
-
-    def block_copy(b, j, send, recv, target):
-        piece = g.at[j, b, pl.ds(0, mb), :]
+    def either(j, action):
+        edge = (j == 0) | (j == nch - 1)
+
+        @pl.when(edge)
+        def _():
+            action(j, WIDTH // 2)
+
+        @pl.when(jnp.logical_not(edge))
+        def _():
+            action(j, WIDTH)
+
+    def chunk(j, width):
+        start = jnp.maximum(j * WIDTH - WIDTH // 2, 0)
+        return pl.ds(pl.multiple_of(start, WIDTH // 2), width)
+
+    def block_copy(b, j, width, send, recv, target):
+        piece = g.at[j, b, pl.ds(0, mb), pl.ds(0, width)]
         return pltpu.make_async_remote_copy(
             src_ref=piece, dst_ref=piece, send_sem=send, recv_sem=recv,
             device_id=(target * 2 + y, c), device_id_type=MESH)
 
-    def left_copy(d, j):
-        return block_copy(z + d, j, left_send.at[d, j], left_recv.at[d + 1, j], z - 1)
-
-    def right_copy(d, j):
-        return block_copy(z - d, j, right_send.at[d, j], right_recv.at[d + 1, j], z + 1)
-
-    def arrival(b, j, recv):
-        piece = g.at[j, b, pl.ds(0, mb), :]
+    def left_copy(d, j, width):
+        return block_copy(z + d, j, width, left_send.at[d, j], left_recv.at[d + 1, j], z - 1)
+
+    def right_copy(d, j, width):
+        return block_copy(z - d, j, width, right_send.at[d, j], right_recv.at[d + 1, j], z + 1)
+
+    def arrival(b, j, width, recv):
+        piece = g.at[j, b, pl.ds(0, mb), pl.ds(0, width)]
         return pltpu.make_async_copy(piece, piece, recv)
 
     def rf_rows(index):
@@ -102,9 +114,10 @@
         piece = rfl.at[lax.rem(z + zc - dz, zc), rf_rows(index)]
         return pltpu.make_async_copy(piece, piece, recv)
 
-    def y_copy(j):
-        return pltpu.make_async_remote_copy(
-            src_ref=ysend.at[j], dst_ref=yrecv.at[j],
+    def y_copy(j, width):
+        at = (j, slice(None), pl.ds(0, width))
+        return pltpu.make_async_remote_copy(
+            src_ref=ysend.at[at], dst_ref=yrecv.at[at],
             send_sem=y_send.at[j], recv_sem=y_recv.at[j],
             device_id=(partner, c), device_id_type=MESH)
 
@@ -116,19 +129,53 @@
         at = pl.ds(pl.multiple_of(which * rows, 16), rows)
         return jnp.concatenate([rfl[o, at, :] for o in range(zc)], axis=1)
 
+    def send_own(j, width):
+        own_part = shaped[:, 0:1] * colv[:, chunk(j, width)].astype(jnp.float32)
+        g[j, z, pl.ds(0, mb), pl.ds(0, width)] = own_part.astype(jnp.bfloat16)
+
+        @pl.when(z > 0)
+        def _():
+            left_copy(0, j, width).start()
+
+        @pl.when(z < zc - 1)
+        def _():
+            right_copy(0, j, width).start()
+
+    def hop(d):
+        def action(j, width):
+            @pl.when(z + d < zc)
+            def _():
+                arrival(z + d, j, width, left_recv.at[d, j]).wait()
+                if d < zc - 1:
+                    @pl.when(z > 0)
+                    def _():
+                        left_copy(d, j, width).start()
+
+            @pl.when(z - d >= 0)
+            def _():
+                arrival(z - d, j, width, right_recv.at[d, j]).wait()
+                if d < zc - 1:
+                    @pl.when(z < zc - 1)
+                    def _():
+                        right_copy(d, j, width).start()
+        return action
+
+    def multiply(j, width):
+        rhs = g[j, :, :, pl.ds(0, width)].reshape(zc * kb, width)
+        other = jnp.dot(lhs(1 - y), rhs, preferred_element_type=jnp.float32)
+        ysend[j, :, pl.ds(0, width)] = other.astype(jnp.bfloat16)
+        y_copy(j, width).start()
+        own[:, chunk(j, width)] = jnp.dot(lhs(y), rhs, preferred_element_type=jnp.float32)
+
+    def finish(j, width):
+        at = chunk(j, width)
+        y_copy(j, width).wait_recv()
+        own[:, at] = wv[:, at] + scale * (own[:, at] + yrecv[j, :, pl.ds(0, width)].astype(jnp.float32))
+
     def tick(t, carry):
         @pl.when(t < nch)
         def _():
-            own_part = shaped[:, 0:1] * colv[:, chunk(t)].astype(jnp.float32)
-            g[t, z, pl.ds(0, mb), :] = own_part.astype(jnp.bfloat16)
-
-            @pl.when(z > 0)
-            def _():
-                left_copy(0, t).start()
-
-            @pl.when(z < zc - 1)
-            def _():
-                right_copy(0, t).start()
+            either(t, send_own)
 
         @pl.when(t == 0)
         def _():
@@ -141,21 +188,7 @@
 
             @pl.when((j >= 0) & (j < nch))
             def _():
-                @pl.when(z + d < zc)
-                def _():
-                    arrival(z + d, j, left_recv.at[d, j]).wait()
-                    if d < zc - 1:
-                        @pl.when(z > 0)
-                        def _():
-                            left_copy(d, j).start()
-
-                @pl.when(z - d >= 0)
-                def _():
-                    arrival(z - d, j, right_recv.at[d, j]).wait()
-                    if d < zc - 1:
-                        @pl.when(z < zc - 1)
-                        def _():
-                            right_copy(d, j).start()
+                either(j, hop(d))
 
         @pl.when(t == 1)
         def _():
@@ -182,11 +215,7 @@
 
         @pl.when((jc >= 0) & (jc < nch))
         def _():
-            at = chunk(jc)
-            rhs = g[jc].reshape(zc * kb, WIDTH)
-            ysend[jc] = jnp.dot(lhs(1 - y), rhs, preferred_element_type=jnp.float32).astype(jnp.bfloat16)
-            y_copy(jc).start()
-            own[:, at] = jnp.dot(lhs(y), rhs, preferred_element_type=jnp.float32)
+            either(jc, multiply)
 
         jf = jc - LAG
 
@@ -196,24 +225,25 @@
 
         @pl.when(jf >= 0)
         def _():
-            at = chunk(jf)
-            y_copy(jf).wait_recv()
-            own[:, at] = wv[:, at] + scale * (own[:, at] + yrecv[jf].astype(jnp.float32))
+            either(jf, finish)
 
         return carry
 
     lax.fori_loop(0, nch + zc - 1 + LAG, tick, 0)
 
-    def drain(j, carry):
+    def sent(j, width):
         for d in range(zc - 1):
             @pl.when((z + d < zc) & (z > 0))
             def _():
-                left_copy(d, j).wait_send()
+                left_copy(d, j, width).wait_send()
 
             @pl.when((z - d >= 0) & (z < zc - 1))
             def _():
-                right_copy(d, j).wait_send()
-        y_copy(j).wait_send()
+                right_copy(d, j, width).wait_send()
+        y_copy(j, width).wait_send()
+
+    def drain(j, carry):
+        either(j, sent)
         return carry
 
     lax.fori_loop(0, nch, drain, 0)
@@ -232,7 +262,7 @@
     zc = pop // 2
     rows, cols = weight.shape
     kb = -(-mb // 128) * 128
-    nch = cols // WIDTH
+    nch = cols // WIDTH + 1
     share = 4 if rows % 32 == 0 and lax.axis_size("col") % 4 == 0 else 2
     anywhere = pl.BlockSpec(memory_space=pl.ANY)
     vmem = pl.BlockSpec(memory_space=pltpu.VMEM)

time: 76.7 us -> 76.8 us (level)
  no operation moved by 1% of the time
where the time goes in v1:
time: 76.8 us; the launch traced here: 76.6 us
  Pallas kernels  74.4 us (97%)
  local copies, waits for them, and re-layouts  2.19 us (3%)
    pallas_call x1, Pallas kernels, body(): pl.pallas_call(functools.partial(kernel, zc, members, share), out_shape=p...  74.4 us
    unnamed x1, local copies, waits for them, and re-layouts  2.19 us

profile of v1, /device:TPU:0, one launch (start us, length us, event | category | flops | bytes accessed | tf_op | source)
XLA Modules:
  0.0 76.6 jit_solution(16600867522614592720)
XLA Ops:
  0.0 74.4 %shard_map.46 = f32[288,4096]{1,0:T(8,128)S(1)} custom-call(s32[1,96]{1,0:T(1,128)} %bitcast.3, bf16[96,2304]{1,0:T(8,128)(2,1)} %bitcast.2, bf16[96,4096]{1,0:T(8,128)(2,1)} %col_ref.1, f32[288,4096]{1,0:T(8,128)} %w_ref.1), custom_call_target="tpu_custom_call" | custom-call | flops 1811939328 | bytes 9437184 | tf_op jit(solution)/shard_map/pallas_call | solution.py:270
  74.4 2.2 %copy.6 = f32[288,4096]{1,0:T(8,128)} copy(f32[288,4096]{1,0:T(8,128)S(1)} %shard_map.46) | data formatting | bytes 9437184

commit v2 on v1

--- a/solution.py
+++ b/solution.py
@@ -10,7 +10,7 @@
 
 MESH = pl.DeviceIdType.MESH
 WIDTH = 256
-LAG = 2
+LAG = 5
 
 
 def kernel(zc, members, share, ranks_ref, rft_ref, col_ref, w_ref, own,

time: 76.8 us -> 76.8 us (level)
  no operation moved by 1% of the time
where the time goes in v2:
time: 76.8 us; the launch traced here: 76.6 us
  Pallas kernels  74.4 us (97%)
  local copies, waits for them, and re-layouts  2.19 us (3%)
    pallas_call x1, Pallas kernels, body(): pl.pallas_call(functools.partial(kernel, zc, members, share), out_shape=p...  74.4 us
    unnamed x1, local copies, waits for them, and re-layouts  2.19 us

profile of v2, /device:TPU:0, one launch (start us, length us, event | category | flops | bytes accessed | tf_op | source)
XLA Modules:
  0.0 76.6 jit_solution(8204410577681966536)
XLA Ops:
  0.0 74.4 %shard_map.46 = f32[288,4096]{1,0:T(8,128)S(1)} custom-call(s32[1,96]{1,0:T(1,128)} %bitcast.3, bf16[96,2304]{1,0:T(8,128)(2,1)} %bitcast.2, bf16[96,4096]{1,0:T(8,128)(2,1)} %col_ref.1, f32[288,4096]{1,0:T(8,128)} %w_ref.1), custom_call_target="tpu_custom_call" | custom-call | flops 1811939328 | bytes 9437184 | tf_op jit(solution)/shard_map/pallas_call | solution.py:270
  74.4 2.2 %copy.6 = f32[288,4096]{1,0:T(8,128)} copy(f32[288,4096]{1,0:T(8,128)S(1)} %shard_map.46) | data formatting | bytes 9437184

commit v3 on v1

--- a/solution.py
+++ b/solution.py
@@ -48,11 +48,6 @@
     eye = lax.broadcasted_iota(jnp.int32, (mb, mb), 0) == lax.broadcasted_iota(jnp.int32, (mb, mb), 1)
     rank = jnp.sum(jnp.where(eye, flat, 0.0), axis=1, keepdims=True)
     shaped[...] = jnp.broadcast_to(rank / (members - 1) - 0.5, shaped.shape)
-    for at in range(0, rf_ref.shape[0], 128):
-        tile = rft_ref[:, at:at + 128].astype(jnp.float32)
-        if kb > mb:
-            tile = jnp.concatenate([tile, jnp.zeros((kb - mb, 128), jnp.float32)], axis=0)
-        rf_ref[at:at + 128, :] = tile.T.astype(jnp.bfloat16)
     col_in.wait()
     pl.semaphore_wait(barrier, zc + 1 + (share == 4))
 
@@ -121,10 +116,6 @@
             send_sem=y_send.at[j], recv_sem=y_recv.at[j],
             device_id=(partner, c), device_id_type=MESH)
 
-    for dz in range(1, zc):
-        rf_copy(dz).start()
-    w_in.start()
-
     def lhs(which):
         at = pl.ds(pl.multiple_of(which * rows, 16), rows)
         return jnp.concatenate([rfl[o, at, :] for o in range(zc)], axis=1)
@@ -173,9 +164,9 @@
         own[:, at] = wv[:, at] + scale * (own[:, at] + yrecv[j, :, pl.ds(0, width)].astype(jnp.float32))
 
     def tick(t, carry):
-        @pl.when(t < nch)
-        def _():
-            either(t, send_own)
+        @pl.when(t + 1 < nch)
+        def _():
+            either(t + 1, send_own)
 
         @pl.when(t == 0)
         def _():
@@ -228,6 +219,16 @@
             either(jf, finish)
 
         return carry
+
+    send_own(0, WIDTH // 2)
+    for at in range(0, rf_ref.shape[0], 128):
+        tile = rft_ref[:, at:at + 128].astype(jnp.float32)
+        if kb > mb:
+            tile = jnp.concatenate([tile, jnp.zeros((kb - mb, 128), jnp.float32)], axis=0)
+        rf_ref[at:at + 128, :] = tile.T.astype(jnp.bfloat16)
+    for dz in range(1, zc):
+        rf_copy(dz).start()
+    w_in.start()
 
     lax.fori_loop(0, nch + zc - 1 + LAG, tick, 0)
 

time: 76.8 us -> 77.2 us (level)
  no operation moved by 1% of the time
where the time goes in v3:
time: 77.2 us; the launch traced here: 77 us
  Pallas kernels  74.8 us (97%)
  local copies, waits for them, and re-layouts  2.19 us (3%)
    pallas_call x1, Pallas kernels, body(): pl.pallas_call(functools.partial(kernel, zc, members, share), out_shape=p...  74.8 us
    unnamed x1, local copies, waits for them, and re-layouts  2.19 us

profile of v3, /device:TPU:0, one launch (start us, length us, event | category | flops | bytes accessed | tf_op | source)
XLA Modules:
  0.0 77.0 jit_solution(11711013536334258709)
XLA Ops:
  0.0 74.8 %shard_map.46 = f32[288,4096]{1,0:T(8,128)S(1)} custom-call(s32[1,96]{1,0:T(1,128)} %bitcast.3, bf16[96,2304]{1,0:T(8,128)(2,1)} %bitcast.2, bf16[96,4096]{1,0:T(8,128)(2,1)} %col_ref.1, f32[288,4096]{1,0:T(8,128)} %w_ref.1), custom_call_target="tpu_custom_call" | custom-call | flops 1811939328 | bytes 9437184 | tf_op jit(solution)/shard_map/pallas_call | solution.py:271
  74.8 2.2 %copy.6 = f32[288,4096]{1,0:T(8,128)} copy(f32[288,4096]{1,0:T(8,128)S(1)} %shard_map.46) | data formatting | bytes 9437184
